TPU v7x, 512 devices: a whole 4x8x8 slice. The times are simulated.
512 devices in a mesh: row: 32 (over y, x_lo, core), col: 16 (over x_hi, z).
Axes of the slice: x: 4 (x_hi: 2, x_lo: 2; x = x_hi * 2 + x_lo), y: 8, z: 8, core: 2. Of those that a mesh axis runs over, the one named last changes fastest.
Arguments:
- object_field: float32 [2, 8192, 8192], P(None, 'row', 'col'), may hold values from -6 to 6
- probe_field: float32 [2, 256, 256], replicated, may hold values from -6 to 6
- intensity: float32 [2048, 256, 256], P(('row', 'col')), may hold values from 0.05 to 4
- offsets: int32 [2048, 2], P(('row', 'col')), may hold values from 0 to 8191, as said below
- counts: int32 [512], P(('row', 'col')), may hold values from 1 to 4, as said below
Outputs:
- object_grad: float32 [2, 8192, 8192], P(None, 'row', 'col')
- probe_grad: float32 [2, 256, 256], replicated
Inputs may be any that keep to these rules, and one draw needn't show every extreme that they name: `offsets`: slot j belongs to the device j // 4 in row-major order over row and col, and its upper left corner lies in that device's object tile. `counts`: some device has all 4 slots live.
All inputs are finite; a program needn't handle non-finite values.
Results may differ from a plain program's by a relative error of at most 0.0003.
Values sent between devices are 32-bit elements; how exact they have to be, the bound alone decides.
A program may use at most 64 MiB of HBM per device.

v0:
```python
import functools
import math

import jax
import jax.numpy as jnp
import ml_dtypes
import numpy as np
from jax import lax
from jax.experimental import pallas as pl
from jax.experimental.pallas import tpu as pltpu
from jax.sharding import PartitionSpec as P

MESH = pl.DeviceIdType.MESH
f32 = jnp.float32
bf16 = jnp.bfloat16
stabilizer = 0.01
N = 256
TR = 256
TC = 512
SLOTS = 4
CH = 32


def dft_tables():
    index = np.arange(N)
    angles = (index[:, None] * index[None, :] % N) * (2.0 * np.pi / N)
    c = np.cos(angles) / math.sqrt(N)
    s = np.sin(angles) / math.sqrt(N)
    both = np.stack([np.block([[c, -s], [s, c]]), np.block([[c, s], [-s, c]])]).astype(np.float32)
    high = both.astype(ml_dtypes.bfloat16)
    low = (both - high.astype(np.float32)).astype(ml_dtypes.bfloat16)
    return np.stack([high, low], axis=1)


def rows(start, size):
    return pl.ds(pl.multiple_of(start, 8), size)


def split(value):
    high = value.astype(bf16)
    return high, (value - high.astype(f32)).astype(bf16)


def dot(a, b):
    return jnp.dot(a, b, preferred_element_type=f32)


def kernel(
    nrow, ncol,
    offs, cnt, obj, probe_in, inten_in, tab_in,
    grad_out, pg_out,
    ext, probe, inten, tab, Rs, Rt, Cs, Ct, rvec, cvec, lvec, cmask, Pw, Pc, X, Y, Pj, D, patch, ex, Tc, Uc, G, kbuf, lbuf, rbuf,
    pgl, crecv, H, yrecv, zsrc, zrecv, xbuf, res,
    local_sem, halo_send, halo_recv, core_send, core_recv, y_send, y_recv, z_send, z_recv, x_send, x_recv,
):
    ny, nz = nrow // 4, ncol // 2
    row, col = lax.axis_index("row"), lax.axis_index("col")
    y, x_lo, core = row // 4, (row // 2) % 2, row % 2
    x_hi, z = col // nz, col % nz
    x = x_hi * 2 + x_lo
    has_up, has_down = row > 0, row < nrow - 1
    has_left, has_right = col > 0, col < ncol - 1
    partner = row + 1 - 2 * core

    def y_peer(k):
        return lax.rem(y + k, ny)

    def z_peer(k):
        return lax.rem(z + k, nz)

    def x_peer(k):
        return lax.rem(x + k, 4)

    def y_id(k):
        return (y_peer(k) * 4 + x_lo * 2 + core, col)

    def z_id(k):
        return (row, x_hi * nz + z_peer(k))

    def x_id(k):
        other = x_peer(k)
        return (y * 4 + lax.rem(other, 2) * 2 + core, (other // 2) * nz + z)

    loads = [
        pltpu.make_async_copy(obj, ext.at[:, pl.ds(0, TR), pl.ds(0, TC)], local_sem.at[0]),
        pltpu.make_async_copy(probe_in, probe, local_sem.at[1]),
        pltpu.make_async_copy(inten_in, inten, local_sem.at[2]),
        pltpu.make_async_copy(tab_in, tab, local_sem.at[3]),
    ]
    loads[1].start()

    barrier = pltpu.get_barrier_semaphore()

    def greet(device):
        pl.semaphore_signal(barrier, inc=1, device_id=device, device_id_type=MESH)

    for k in range(1, ny):
        greet(y_id(k))
    for k in range(1, nz):
        greet(z_id(k))
    for k in range(1, 4):
        greet(x_id(k))
    far_right = has_right & (z == nz - 1)
    far_left = has_left & (z == 0)

    @pl.when(has_up)
    def _():
        greet((row - 1, col))

    @pl.when(has_down)
    def _():
        greet((row + 1, col))

    @pl.when(far_left)
    def _():
        greet((row, col - 1))

    @pl.when(far_right)
    def _():
        greet((row, col + 1))

    loads[0].start()
    loads[2].start()
    loads[3].start()
    one = lambda flag: flag.astype(jnp.int32)
    pl.semaphore_wait(barrier, ny + nz + 1 + one(has_up) + one(has_down) + one(far_left) + one(far_right))

    def halo(index, source, target, device):
        return pltpu.make_async_remote_copy(
            src_ref=source, dst_ref=target, send_sem=halo_send.at[index], recv_sem=halo_recv.at[index],
            device_id=device, device_id_type=MESH,
        )

    up_id = (lax.max(row - 1, 0), col)
    down_id = (lax.min(row + 1, nrow - 1), col)
    left_id = (row, lax.max(col - 1, 0))
    right_id = (row, lax.min(col + 1, ncol - 1))
    top, bottom = pl.ds(0, TR), pl.ds(TR, TR)
    main, side = pl.ds(0, TC), pl.ds(TC, N)
    right_in = halo(0, obj.at[:, :, pl.ds(0, N)], ext.at[:, top, side], left_id)
    lower_in = halo(1, obj, ext.at[:, bottom, main], up_id)
    corner_in = halo(2, ext.at[:, top, side], ext.at[:, bottom, side], up_id)

    @pl.when(has_left)
    def _():
        right_in.start()

    @pl.when(has_up)
    def _():
        lower_in.start()

    @pl.when(jnp.logical_not(has_right))
    def _():
        ext[:, :, TC:] = jnp.zeros((2, 2 * TR, N), f32)

    @pl.when(jnp.logical_not(has_down))
    def _():
        ext[:, TR:, :] = jnp.zeros((2, TR, TC + N), f32)

    @pl.when(jnp.logical_not(has_up))
    def _():
        kbuf[...] = jnp.zeros_like(kbuf)
        lbuf[...] = jnp.zeros_like(lbuf)

    @pl.when(jnp.logical_not(has_left))
    def _():
        rbuf[...] = jnp.zeros_like(rbuf)

    lanes = lax.broadcasted_iota(jnp.int32, (CH, N), 1)
    lines = lax.broadcasted_iota(jnp.int32, (CH, N), 0)

    def one_hot(flag):
        return jnp.where(flag, 1.0, 0.0).astype(bf16)

    for s in range(SLOTS):
        r = jnp.full((CH, N), offs[s, 0], jnp.int32) - row * TR
        c = jnp.full((CH, N), offs[s, 1], jnp.int32) - col * TC
        rvec[s] = r
        cvec[s] = c
        lvec[s] = jnp.where(jnp.full((CH, N), cnt[0], jnp.int32) > s, 1.0, 0.0)
        for b in range(3):
            cmask[s, b] = jnp.where((lanes + N * b >= c) & (lanes + N * b < c + N), 1.0, 0.0)[:8]

    def permutations(s, _):
        r, c = rvec[s], cvec[s]

        def body(i, _):
            line = lines + i * CH
            Rs[s, rows(i * CH, CH), :] = one_hot(line == ((lanes + r) & (N - 1)))
            Rt[s, rows(i * CH, CH), :] = one_hot(lanes == ((line + r) & (N - 1)))
            Cs[s, rows(i * CH, CH), :] = one_hot(lanes == ((line + c) & (N - 1)))
            Ct[s, rows(i * CH, CH), :] = one_hot(line == ((lanes + c) & (N - 1)))
            return 0

        lax.fori_loop(0, N // CH, body, 0)
        return 0

    lax.fori_loop(0, SLOTS, permutations, 0)

    loads[1].wait()

    def split_probe(i, _):
        here = rows(i * CH, CH)
        for q in range(2):
            high, low = split(probe[q, here, :])
            Pw[here, q * N:(q + 1) * N] = high
            Pw[here, (q + 2) * N:(q + 3) * N] = low
        return 0

    lax.fori_loop(0, N // CH, split_probe, 0)

    def shift_probe(s, _):
        a = dot(Rs[s], Pw[...])
        for p in range(4):
            Uc[p * N:(p + 1) * N, :] = a[:, p * N:(p + 1) * N].astype(bf16)
        a = dot(Uc[...], Cs[s])
        for q in range(2):
            Pc[s, q] = a[q * N:(q + 1) * N] + a[(q + 2) * N:(q + 3) * N]
        return 0

    lax.fori_loop(0, SLOTS, shift_probe, 0)

    @pl.when(has_right)
    def _():
        right_in.wait_recv()

        @pl.when(has_up)
        def _():
            corner_in.start()

    for load in (loads[0], loads[2], loads[3]):
        load.wait()

    @pl.when(has_down)
    def _():
        lower_in.wait_recv()

        @pl.when(has_right)
        def _():
            corner_in.wait_recv()

    def slot(s, _):
        def gather(i, _):
            i0 = i * CH
            from_below = lines + i0 < rvec[s]
            first, second = lanes >= cvec[s], lanes + N >= cvec[s]
            parts = []
            for q in range(2):
                u = ext[q, rows(i0, CH), :]
                v = ext[q, rows(i0 + TR, CH), :]
                blocks = [jnp.where(from_below, v[:, b * N:(b + 1) * N], u[:, b * N:(b + 1) * N]) for b in range(3)]
                w = jnp.where(first, blocks[0], jnp.where(second, blocks[1], blocks[2]))
                patch[s, q, rows(i0, CH), :] = w
                parts.append(w)
            pr, pi = Pc[s, 0, rows(i0, CH), :], Pc[s, 1, rows(i0, CH), :]
            waves = (pr * parts[0] - pi * parts[1], pr * parts[1] + pi * parts[0])
            for q, wave in enumerate(waves):
                ex[s, q, rows(i0, CH), :] = wave
                high, low = split(wave)
                X[s, rows(i0, CH), q * N:(q + 1) * N] = high
                X[s, rows(i0 + N, CH), q * N:(q + 1) * N] = low
            return 0

        lax.fori_loop(0, N // CH, gather, 0, unroll=8)
        a = dot(X[s], tab[0, 0])
        a = a[:N] + a[N:] + dot(X[s, :N], tab[0, 1])
        for q in range(2):
            high, low = split(a[:, q * N:(q + 1) * N])
            Y[s, q * N:(q + 1) * N, :N] = high
            Y[s, q * N:(q + 1) * N, N:] = low
        a = dot(tab[1, 0], Y[s])
        D[s] = a[:, :N] + a[:, N:] + dot(tab[1, 1], Y[s, :, :N])

        def project(i, _):
            i0 = i * CH
            zr, zi = D[s, rows(i0, CH), :], D[s, rows(i0 + N, CH), :]
            measured = inten[s, rows(i0, CH), :]
            factor = measured * lax.rsqrt(measured * (zr * zr + zi * zi + stabilizer))
            for q, wave in enumerate((zr * factor, zi * factor)):
                high, low = split(wave)
                Pj[s, rows(i0 + q * N, CH), :N] = high
                Pj[s, rows(i0 + q * N, CH), N:] = low
            return 0

        lax.fori_loop(0, N // CH, project, 0, unroll=8)
        a = dot(tab[0, 0], Pj[s])
        a = a[:, :N] + a[:, N:] + dot(tab[0, 1], Pj[s, :, :N])
        for q in range(2):
            high, low = split(a[q * N:(q + 1) * N])
            X[s, :N, q * N:(q + 1) * N] = high
            X[s, N:, q * N:(q + 1) * N] = low
        a = dot(X[s], tab[1, 0])
        a = a[:N] + a[N:] + dot(X[s, :N], tab[1, 1])
        D[s, :N] = a[:, :N]
        D[s, N:] = a[:, N:]

        def finish(i, _):
            i0 = i * CH
            here, below = rows(i0, CH), rows(i0 + N, CH)
            live = lvec[s]
            dr = (ex[s, 0, here, :] - D[s, here, :]) * live
            di = (ex[s, 1, here, :] - D[s, below, :]) * live
            wr, wi = patch[s, 0, here, :], patch[s, 1, here, :]
            for q, term in enumerate((wr * dr + wi * di, wr * di - wi * dr)):
                high, low = split(term)
                Tc[here, q * N:(q + 1) * N] = high
                Tc[here, (q + 2) * N:(q + 3) * N] = low
            pr, pi = Pc[s, 0, here, :], Pc[s, 1, here, :]
            ex[s, 0, here, :] = pr * dr + pi * di
            ex[s, 1, here, :] = pr * di - pi * dr
            return 0

        lax.fori_loop(0, N // CH, finish, 0, unroll=8)

        a = dot(Rt[s], Tc[...])
        for q in range(2):
            high, low = split(a[:, q * N:(q + 1) * N] + a[:, (q + 2) * N:(q + 3) * N])
            Uc[q * N:(q + 1) * N, :] = high
            Uc[(q + 2) * N:(q + 3) * N, :] = low
        a = dot(Uc[...], Ct[s])
        for q in range(2):
            pgl[q] += a[q * N:(q + 1) * N] + a[(q + 2) * N:(q + 3) * N]
        return 0

    pgl[...] = jnp.zeros_like(pgl)
    lax.fori_loop(0, SLOTS, slot, 0)

    def deposit(i, _):
        i0 = i * 8
        here, below = rows(i0, 8), rows(i0 + N, 8)
        for q in range(2):
            terms = [ex[s, q, here, :] for s in range(SLOTS)]
            lower = [jnp.where(lines[:8] + i0 < rvec[s, :8], terms[s], 0.0) for s in range(SLOTS)]
            upper = [terms[s] - lower[s] for s in range(SLOTS)]
            for b in range(3):
                for part, target in ((lower, below), (upper, here)):
                    kept = [part[s] * cmask[s, b] for s in range(SLOTS)]
                    G[q, target, b * N:(b + 1) * N] = (kept[0] + kept[1]) + (kept[2] + kept[3])
        return 0

    lax.fori_loop(0, N // 8, deposit, 0, unroll=4)

    corner_out = halo(3, G.at[:, bottom, side], kbuf, down_id)
    lower_out = halo(4, G.at[:, bottom, main], lbuf, down_id)
    right_out = halo(5, G.at[:, top, side], rbuf, right_id)

    @pl.when(has_down)
    def _():
        corner_out.start()
        lower_out.start()

    def remote(source, target, send, recv, device):
        return pltpu.make_async_remote_copy(
            src_ref=source, dst_ref=target, send_sem=send, recv_sem=recv, device_id=device, device_id_type=MESH
        )

    to_partner = remote(pgl.at[1 - core], crecv, core_send.at[0], core_recv.at[0], (partner, col))
    to_partner.start()
    to_partner.wait_recv()

    def add_core(i, _):
        H[rows(i * CH, CH), :] = pgl[core, rows(i * CH, CH), :] + crecv[rows(i * CH, CH), :]
        return 0

    lax.fori_loop(0, N // CH, add_core, 0, unroll=8)
    ystep = N // ny
    y_out = [
        remote(H.at[rows(y_peer(k) * ystep, ystep), :], yrecv.at[k], y_send.at[k], y_recv.at[k], y_id(k)) for k in range(1, ny)
    ]
    for copy in y_out:
        copy.start()

    @pl.when(has_up)
    def _():
        corner_out.wait_recv()

    def add_corner(i, _):
        for q in range(2):
            G[q, rows(i * CH, CH), TC:] += kbuf[q, rows(i * CH, CH), :]
        return 0

    lax.fori_loop(0, TR // CH, add_corner, 0, unroll=8)

    @pl.when(has_right)
    def _():
        right_out.start()

    for copy in y_out:
        copy.wait_recv()
    summed = H[rows(y * ystep, ystep), :]
    for k in range(1, ny):
        summed = summed + yrecv[k]
    for p in range(nz):
        zsrc[p] = summed[8 * (p // 2):8 * (p // 2) + 8, 128 * (p % 2):128 * (p % 2) + 128]
    z_out = [remote(zsrc.at[z_peer(k)], zrecv.at[k], z_send.at[k], z_recv.at[k], z_id(k)) for k in range(1, nz)]
    for copy in z_out:
        copy.start()
    for copy in z_out:
        copy.wait_recv()
    tile = zsrc[z]
    for k in range(1, nz):
        tile = tile + zrecv[k]
    xbuf[x] = tile
    x_out = [remote(xbuf.at[x], xbuf.at[x], x_send.at[k], x_recv.at[k], x_id(k)) for k in range(1, 4)]
    for copy in x_out:
        copy.start()
    for copy in x_out:
        copy.wait_recv()
    tile = ((xbuf[0] + xbuf[1]) + (xbuf[2] + xbuf[3])) * f32(1.0 / math.sqrt(SLOTS * nrow * ncol))
    my_tile = (core, rows(y * ystep + 8 * (z // 2), 8), pl.ds(pl.multiple_of(128 * (z % 2), 128), 128))
    res[my_tile] = tile
    z_back = [remote(res.at[my_tile], res.at[my_tile], z_send.at[nz + k], z_recv.at[nz + k], z_id(k)) for k in range(1, nz)]
    for copy in z_back:
        copy.start()
    for copy in z_back:
        copy.wait_recv()
    my_rows = (core, rows(y * ystep, ystep))
    y_back = [remote(res.at[my_rows], res.at[my_rows], y_send.at[ny + k], y_recv.at[ny + k], y_id(k)) for k in range(1, ny)]
    for copy in y_back:
        copy.start()
    for copy in y_back:
        copy.wait_recv()
    share = remote(res.at[core], res.at[core], core_send.at[1], core_recv.at[1], (partner, col))
    share.start()

    @pl.when(has_up)
    def _():
        lower_out.wait_recv()

    @pl.when(has_left)
    def _():
        right_out.wait_recv()

    def add_halos(i, _):
        here = rows(i * CH, CH)
        for q in range(2):
            G[q, here, :N] = G[q, here, :N] + lbuf[q, here, :N] + rbuf[q, here, :]
            G[q, here, N:TC] = G[q, here, N:TC] + lbuf[q, here, N:]
        return 0

    lax.fori_loop(0, TR // CH, add_halos, 0, unroll=8)
    store_grad = pltpu.make_async_copy(G.at[:, top, main], grad_out, local_sem.at[4])
    store_grad.start()
    share.wait_recv()
    store_probe = pltpu.make_async_copy(res, pg_out, local_sem.at[5])
    store_probe.start()

    @pl.when(has_left)
    def _():
        right_in.wait_send()

    @pl.when(has_up)
    def _():
        lower_in.wait_send()

        @pl.when(has_right)
        def _():
            corner_in.wait_send()

    @pl.when(has_down)
    def _():
        corner_out.wait_send()
        lower_out.wait_send()

    @pl.when(has_right)
    def _():
        right_out.wait_send()

    to_partner.wait_send()
    share.wait_send()
    for copy in y_out + z_out + x_out + z_back + y_back:
        copy.wait_send()
    store_grad.wait()
    store_probe.wait()


def local(nrow, ncol, object_field, probe_field, intensity, offsets, counts):
    ny, nz = nrow // 4, ncol // 2
    anywhere = pl.BlockSpec(memory_space=pl.ANY)
    scalars = pl.BlockSpec(memory_space=pltpu.SMEM)
    vmem = pltpu.VMEM
    dma = pltpu.SemaphoreType.DMA
    grad, probe_grad = pl.pallas_call(
        functools.partial(kernel, nrow, ncol),
        out_shape=[jax.ShapeDtypeStruct((2, TR, TC), f32), jax.ShapeDtypeStruct((2, N, N), f32)],
        in_specs=[scalars, scalars] + [anywhere] * 4,
        out_specs=[anywhere, anywhere],
        scratch_shapes=[
            vmem((2, 2 * TR, TC + N), f32),
            vmem((2, N, N), f32),
            vmem((SLOTS, N, N), f32),
            vmem((2, 2, 2 * N, 2 * N), bf16),
            vmem((SLOTS, N, N), bf16),
            vmem((SLOTS, N, N), bf16),
            vmem((SLOTS, N, N), bf16),
            vmem((SLOTS, N, N), bf16),
            vmem((SLOTS, CH, N), jnp.int32),
            vmem((SLOTS, CH, N), jnp.int32),
            vmem((SLOTS, CH, N), f32),
            vmem((SLOTS, 3, 8, N), f32),
            vmem((N, 4 * N), bf16),
            vmem((SLOTS, 2, N, N), f32),
            vmem((SLOTS, 2 * N, 2 * N), bf16),
            vmem((SLOTS, 2 * N, 2 * N), bf16),
            vmem((SLOTS, 2 * N, 2 * N), bf16),
            vmem((SLOTS, 2 * N, N), f32),
            vmem((SLOTS, 2, N, N), f32),
            vmem((SLOTS, 2, N, N), f32),
            vmem((N, 4 * N), bf16),
            vmem((4 * N, N), bf16),
            vmem((2, 2 * TR, TC + N), f32),
            vmem((2, TR, N), f32),
            vmem((2, TR, TC), f32),
            vmem((2, TR, N), f32),
            vmem((2, N, N), f32),
            vmem((N, N), f32),
            vmem((N, N), f32),
            vmem((ny, N // ny, N), f32),
            vmem((nz, 8, 128), f32),
            vmem((nz, 8, 128), f32),
            vmem((4, 8, 128), f32),
            vmem((2, N, N), f32),
            dma((6,)), dma((6,)), dma((6,)), dma((2,)), dma((2,)),
            dma((2 * ny,)), dma((2 * ny,)), dma((2 * nz,)), dma((2 * nz,)), dma((4,)), dma((4,)),
        ],
        compiler_params=pltpu.CompilerParams(collective_id=0, has_side_effects=True, vmem_limit_bytes=56 * 2**20),
    )(offsets, counts, object_field, probe_field, intensity, jnp.asarray(dft_tables()))
    return grad, probe_grad


def solution(mesh):
    in_specs = (
        P(None, "row", "col"),
        P(),
        P(("row", "col"), None, None),
        P(("row", "col"), None),
        P(("row", "col")),
    )
    out_specs = (P(None, "row", "col"), P())
    body = functools.partial(local, mesh.shape["row"], mesh.shape["col"])
    return jax.shard_map(body, mesh=mesh, in_specs=in_specs, out_specs=out_specs, check_vma=False)
```

profile of v0, /device:TPU:1, one launch (start us, length us, event | category | flops | bytes accessed | tf_op | source)
XLA Modules:
  0.0 110.2 jit_solution(11686040489595252046)
XLA Ops:
  1.3 1.3 %copy.8.offs = s32[4,2]{1,0:T(4,128)} copy(s32[4,2]{0,1:T(2,128)} %param.9) | data formatting | bytes 64 | tf_op args[3]
  2.6 104.5 %shard_map.77 = (f32[2,256,512]{2,1,0:T(8,128)}, f32[2,256,256]{2,1,0:T(8,128)}) custom-call(s32[4,2]{1,0:T(4,128)} %copy.8.offs, s32[1]{0:T(128)S(6)} %copy.11.cnt, f32[2,256,512]{2,1,0:T(8,128)} %obj.1, f32[2,256,256]{2,1,0:T(8,128)} %probe_in.1, f32[4,256,256]{2,1,0:T(8,128)} %inten_in.1, bf16[2,2,512,512]{3,2,1,0:T(8,128)(2,1)} %constant.2.clone.tab_in), custom_call_target="tpu_custom_call" | custom-call | tf_op jit(solution)/shard_map/pallas_call | solution.py:483
  107.1 0.0 copy-start
  107.1 2.3 %copy.12 = f32[2,256,512]{2,1,0:T(8,128)} copy(f32[2,256,512]{2,1,0:T(8,128)} %get-tuple-element.4) | data formatting | bytes 2097152
  109.4 0.0 copy-done
  109.4 0.8 copy.13
Async XLA Ops:
  107.1 2.3 %copy-start = (f32[2,256,256]{2,1,0:T(8,128)S(1)}, f32[2,256,256]{2,1,0:T(8,128)}, u32[]{:S(2)}) copy-start(f32[2,256,256]{2,1,0:T(8,128)} %get-tuple-element.5) | copy-start | bytes 1572868
where the time goes:
time: 110 us
  Pallas kernels  104 us (95%)
  local copies, waits for them, and re-layouts  4.45 us (4%)
  between operations  1.29 us (1%)
    pallas_call x1, Pallas kernels, local(): pl.pallas_call(functools.partial(kernel, nrow, ncol), out_shape=[jax.Shap...  104 us
    unnamed x5, local copies, waits for them, and re-layouts  4.45 us

commit v1 on v0

--- a/solution.py
+++ b/solution.py
@@ -50,7 +50,7 @@
     offs, cnt, obj, probe_in, inten_in, tab_in,
     grad_out, pg_out,
     ext, probe, inten, tab, Rs, Rt, Cs, Ct, rvec, cvec, lvec, cmask, Pw, Pc, X, Y, Pj, D, patch, ex, Tc, Uc, G, kbuf, lbuf, rbuf,
-    pgl, crecv, H, yrecv, zsrc, zrecv, xbuf, res,
+    pgl, crecv, H, zrecv, ysrc, yrecv, xbuf, res,
     local_sem, halo_send, halo_recv, core_send, core_recv, y_send, y_recv, z_send, z_recv, x_send, x_recv,
 ):
     ny, nz = nrow // 4, ncol // 2
@@ -137,13 +137,19 @@
     right_id = (row, lax.min(col + 1, ncol - 1))
     top, bottom = pl.ds(0, TR), pl.ds(TR, TR)
     main, side = pl.ds(0, TC), pl.ds(TC, N)
-    right_in = halo(0, obj.at[:, :, pl.ds(0, N)], ext.at[:, top, side], left_id)
+    half = TR // 2
+    halves = (pl.ds(0, half), pl.ds(half, half))
+    right_in = [
+        halo(0, obj.at[:, halves[0], pl.ds(0, N)], ext.at[:, halves[0], side], left_id),
+        halo(6, obj.at[:, halves[1], pl.ds(0, N)], ext.at[:, halves[1], side], left_id),
+    ]
     lower_in = halo(1, obj, ext.at[:, bottom, main], up_id)
     corner_in = halo(2, ext.at[:, top, side], ext.at[:, bottom, side], up_id)
 
     @pl.when(has_left)
     def _():
-        right_in.start()
+        right_in[0].start()
+        right_in[1].start()
 
     @pl.when(has_up)
     def _():
@@ -173,8 +179,8 @@
         return jnp.where(flag, 1.0, 0.0).astype(bf16)
 
     for s in range(SLOTS):
-        r = jnp.full((CH, N), offs[s, 0], jnp.int32) - row * TR
-        c = jnp.full((CH, N), offs[s, 1], jnp.int32) - col * TC
+        r = jnp.full((CH, N), offs[0, s], jnp.int32) - row * TR
+        c = jnp.full((CH, N), offs[1, s], jnp.int32) - col * TC
         rvec[s] = r
         cvec[s] = c
         lvec[s] = jnp.where(jnp.full((CH, N), cnt[0], jnp.int32) > s, 1.0, 0.0)
@@ -222,7 +228,8 @@
 
     @pl.when(has_right)
     def _():
-        right_in.wait_recv()
+        right_in[0].wait_recv()
+        right_in[1].wait_recv()
 
         @pl.when(has_up)
         def _():
@@ -325,6 +332,14 @@
     pgl[...] = jnp.zeros_like(pgl)
     lax.fori_loop(0, SLOTS, slot, 0)
 
+    def remote(source, target, send, recv, device):
+        return pltpu.make_async_remote_copy(
+            src_ref=source, dst_ref=target, send_sem=send, recv_sem=recv, device_id=device, device_id_type=MESH
+        )
+
+    to_partner = remote(pgl.at[1 - core], crecv, core_send.at[0], core_recv.at[0], (partner, col))
+    to_partner.start()
+
     def deposit(i, _):
         i0 = i * 8
         here, below = rows(i0, 8), rows(i0 + N, 8)
@@ -342,34 +357,40 @@
 
     corner_out = halo(3, G.at[:, bottom, side], kbuf, down_id)
     lower_out = halo(4, G.at[:, bottom, main], lbuf, down_id)
-    right_out = halo(5, G.at[:, top, side], rbuf, right_id)
+    right_out = [
+        halo(5, G.at[:, halves[0], side], rbuf.at[:, halves[0], :], right_id),
+        halo(8, G.at[:, halves[1], side], rbuf.at[:, halves[1], :], right_id),
+    ]
 
     @pl.when(has_down)
     def _():
         corner_out.start()
         lower_out.start()
 
-    def remote(source, target, send, recv, device):
-        return pltpu.make_async_remote_copy(
-            src_ref=source, dst_ref=target, send_sem=send, recv_sem=recv, device_id=device, device_id_type=MESH
-        )
-
-    to_partner = remote(pgl.at[1 - core], crecv, core_send.at[0], core_recv.at[0], (partner, col))
-    to_partner.start()
     to_partner.wait_recv()
 
     def add_core(i, _):
-        H[rows(i * CH, CH), :] = pgl[core, rows(i * CH, CH), :] + crecv[rows(i * CH, CH), :]
-        return 0
-
-    lax.fori_loop(0, N // CH, add_core, 0, unroll=8)
-    ystep = N // ny
-    y_out = [
-        remote(H.at[rows(y_peer(k) * ystep, ystep), :], yrecv.at[k], y_send.at[k], y_recv.at[k], y_id(k)) for k in range(1, ny)
-    ]
+        for p in range(nz):
+            here = rows(i * nz * 8 + p * 8, 8)
+            H[i, p] = pgl[core, here, :] + crecv[here, :]
+        return 0
+
+    lax.fori_loop(0, N // (8 * nz), add_core, 0, unroll=True)
+    z_out = [remote(H.at[:, z_peer(k)], zrecv.at[k], z_send.at[k], z_recv.at[k], z_id(k)) for k in range(1, nz)]
+    for copy in z_out:
+        copy.start()
+
+    for copy in z_out:
+        copy.wait_recv()
+    for a in range(N // (8 * nz)):
+        summed = H[a, z]
+        for k in range(1, nz):
+            summed = summed + zrecv[k, a]
+        for half in range(2):
+            ysrc[2 * a + half] = summed[:, 128 * half:128 * half + 128]
+    y_out = [remote(ysrc.at[y_peer(k)], yrecv.at[k], y_send.at[k], y_recv.at[k], y_id(k)) for k in range(1, ny)]
     for copy in y_out:
         copy.start()
-
     @pl.when(has_up)
     def _():
         corner_out.wait_recv()
@@ -383,23 +404,14 @@
 
     @pl.when(has_right)
     def _():
-        right_out.start()
+        right_out[0].start()
+        right_out[1].start()
 
     for copy in y_out:
         copy.wait_recv()
-    summed = H[rows(y * ystep, ystep), :]
+    tile = ysrc[y]
     for k in range(1, ny):
-        summed = summed + yrecv[k]
-    for p in range(nz):
-        zsrc[p] = summed[8 * (p // 2):8 * (p // 2) + 8, 128 * (p % 2):128 * (p % 2) + 128]
-    z_out = [remote(zsrc.at[z_peer(k)], zrecv.at[k], z_send.at[k], z_recv.at[k], z_id(k)) for k in range(1, nz)]
-    for copy in z_out:
-        copy.start()
-    for copy in z_out:
-        copy.wait_recv()
-    tile = zsrc[z]
-    for k in range(1, nz):
-        tile = tile + zrecv[k]
+        tile = tile + yrecv[k]
     xbuf[x] = tile
     x_out = [remote(xbuf.at[x], xbuf.at[x], x_send.at[k], x_recv.at[k], x_id(k)) for k in range(1, 4)]
     for copy in x_out:
@@ -407,14 +419,16 @@
     for copy in x_out:
         copy.wait_recv()
     tile = ((xbuf[0] + xbuf[1]) + (xbuf[2] + xbuf[3])) * f32(1.0 / math.sqrt(SLOTS * nrow * ncol))
-    my_tile = (core, rows(y * ystep + 8 * (z // 2), 8), pl.ds(pl.multiple_of(128 * (z % 2), 128), 128))
+    my_lanes = pl.ds(pl.multiple_of(128 * (y % 2), 128), 128)
+    my_tile = (core, rows(8 * nz * (y // 2) + 8 * z, 8), my_lanes)
     res[my_tile] = tile
     z_back = [remote(res.at[my_tile], res.at[my_tile], z_send.at[nz + k], z_recv.at[nz + k], z_id(k)) for k in range(1, nz)]
     for copy in z_back:
         copy.start()
+
     for copy in z_back:
         copy.wait_recv()
-    my_rows = (core, rows(y * ystep, ystep))
+    my_rows = (core, rows(8 * nz * (y // 2), 8 * nz), my_lanes)
     y_back = [remote(res.at[my_rows], res.at[my_rows], y_send.at[ny + k], y_recv.at[ny + k], y_id(k)) for k in range(1, ny)]
     for copy in y_back:
         copy.start()
@@ -429,7 +443,8 @@
 
     @pl.when(has_left)
     def _():
-        right_out.wait_recv()
+        right_out[0].wait_recv()
+        right_out[1].wait_recv()
 
     def add_halos(i, _):
         here = rows(i * CH, CH)
@@ -447,7 +462,8 @@
 
     @pl.when(has_left)
     def _():
-        right_in.wait_send()
+        right_in[0].wait_send()
+        right_in[1].wait_send()
 
     @pl.when(has_up)
     def _():
@@ -464,7 +480,8 @@
 
     @pl.when(has_right)
     def _():
-        right_out.wait_send()
+        right_out[0].wait_send()
+        right_out[1].wait_send()
 
     to_partner.wait_send()
     share.wait_send()
@@ -514,17 +531,17 @@
             vmem((2, TR, N), f32),
             vmem((2, N, N), f32),
             vmem((N, N), f32),
-            vmem((N, N), f32),
-            vmem((ny, N // ny, N), f32),
-            vmem((nz, 8, 128), f32),
-            vmem((nz, 8, 128), f32),
+            vmem((N // (8 * nz), nz, 8, N), f32),
+            vmem((nz, N // (8 * nz), 8, N), f32),
+            vmem((ny, 8, 128), f32),
+            vmem((ny, 8, 128), f32),
             vmem((4, 8, 128), f32),
             vmem((2, N, N), f32),
-            dma((6,)), dma((6,)), dma((6,)), dma((2,)), dma((2,)),
+            dma((6,)), dma((9,)), dma((9,)), dma((2,)), dma((2,)),
             dma((2 * ny,)), dma((2 * ny,)), dma((2 * nz,)), dma((2 * nz,)), dma((4,)), dma((4,)),
         ],
         compiler_params=pltpu.CompilerParams(collective_id=0, has_side_effects=True, vmem_limit_bytes=56 * 2**20),
-    )(offsets, counts, object_field, probe_field, intensity, jnp.asarray(dft_tables()))
+    )(offsets.T, counts, object_field, probe_field, intensity, jnp.asarray(dft_tables()))
     return grad, probe_grad
 
 

time: 110 us -> 102 us (0.927)
  Pallas kernels: 104 us -> 97.2 us
  local copies, waits for them, and re-layouts: 4.45 us -> 3.12 us
    pallas_call x1, Pallas kernels: 104 us -> 97.2 us  [local(): pl.pallas_call(functools.partial(kernel, nrow, ncol), out_shape=[jax.Shap...]
    unnamed x5 -> x4, local copies, waits for them, and re-layouts: 4.45 us -> 3.12 us
where the time goes in v1:
time: 102 us
  Pallas kernels  97.2 us (95%)
  local copies, waits for them, and re-layouts  3.12 us (3%)
  between operations  1.29 us (1%)
    pallas_call x1, Pallas kernels, local(): pl.pallas_call(functools.partial(kernel, nrow, ncol), out_shape=[jax.Shap...  97.2 us
    unnamed x4, local copies, waits for them, and re-layouts  3.12 us

profile of v1, /device:TPU:1, one launch (start us, length us, event | category | flops | bytes accessed | tf_op | source)
XLA Modules:
  0.0 101.6 jit_solution(3681604949858728857)
XLA Ops:
  1.3 97.2 %shard_map.77 = (f32[2,256,512]{2,1,0:T(8,128)}, f32[2,256,256]{2,1,0:T(8,128)}) custom-call(s32[2,4]{1,0:T(2,128)} %bitcast.1, s32[1]{0:T(128)S(6)} %copy.10.cnt, f32[2,256,512]{2,1,0:T(8,128)} %obj.1, f32[2,256,256]{2,1,0:T(8,128)} %probe_in.1, f32[4,256,256]{2,1,0:T(8,128)} %inten_in.1, bf16[2,2,512,512]{3,2,1,0:T(8,128)(2,1)} %constant.2.clone.tab_in), custom_call_target="tpu_custom_call" | custom-call | tf_op jit(solution)/shard_map/pallas_call | solution.py:500
  98.5 0.0 copy-start
  98.5 2.3 %copy.11 = f32[2,256,512]{2,1,0:T(8,128)} copy(f32[2,256,512]{2,1,0:T(8,128)} %get-tuple-element.4) | data formatting | bytes 2097152
  100.8 0.0 copy-done
  100.8 0.8 copy.12
Async XLA Ops:
  98.5 2.3 %copy-start = (f32[2,256,256]{2,1,0:T(8,128)S(1)}, f32[2,256,256]{2,1,0:T(8,128)}, u32[]{:S(2)}) copy-start(f32[2,256,256]{2,1,0:T(8,128)} %get-tuple-element.5) | copy-start | bytes 1572868

commit v2 on v1

--- a/solution.py
+++ b/solution.py
@@ -19,11 +19,12 @@
 TC = 512
 SLOTS = 4
 CH = 32
+M = N // 2
 
 
 def dft_tables():
-    index = np.arange(N)
-    angles = (index[:, None] * index[None, :] % N) * (2.0 * np.pi / N)
+    index = np.arange(M)
+    angles = (index[:, None] * index[None, :] % M) * (2.0 * np.pi / M)
     c = np.cos(angles) / math.sqrt(N)
     s = np.sin(angles) / math.sqrt(N)
     both = np.stack([np.block([[c, -s], [s, c]]), np.block([[c, s], [-s, c]])]).astype(np.float32)
@@ -32,6 +33,12 @@
     return np.stack([high, low], axis=1)
 
 
+def twiddles():
+    angles = np.arange(M) * (2.0 * np.pi / N)
+    pair = np.stack([np.cos(angles), np.sin(angles)]).astype(np.float32)
+    return np.broadcast_to(pair[:, :, None], (2, M, N)).copy(), np.broadcast_to(pair[:, None, :], (2, N, M)).copy()
+
+
 def rows(start, size):
     return pl.ds(pl.multiple_of(start, 8), size)
 
@@ -45,11 +52,22 @@
     return jnp.dot(a, b, preferred_element_type=f32)
 
 
+def forward_half(tops, bottoms, cosine, sine):
+    real, imag = tops[0] - bottoms[0], tops[1] - bottoms[1]
+    odd = (real * cosine + imag * sine, imag * cosine - real * sine)
+    return (tops[0] + bottoms[0], tops[1] + bottoms[1]), odd
+
+
+def backward_half(even, odd, cosine, sine):
+    real, imag = odd[0] * cosine - odd[1] * sine, odd[0] * sine + odd[1] * cosine
+    return (even[0] + real, even[1] + imag), (even[0] - real, even[1] - imag)
+
+
 def kernel(
     nrow, ncol,
-    offs, cnt, obj, probe_in, inten_in, tab_in,
+    offs, cnt, obj, probe_in, inten_in, tab_in, row_turn_in, lane_turn_in,
     grad_out, pg_out,
-    ext, probe, inten, tab, Rs, Rt, Cs, Ct, rvec, cvec, lvec, cmask, Pw, Pc, X, Y, Pj, D, patch, ex, Tc, Uc, G, kbuf, lbuf, rbuf,
+    ext, probe, inten, tab, row_turn, lane_turn, Ip, Rs, Rt, Cs, Ct, rvec, cvec, lvec, cmask, Pw, Pc, X, Y, Pj, D, B, patch, ex, Tc, Uc, G, kbuf, lbuf, rbuf,
     pgl, crecv, H, zrecv, ysrc, yrecv, xbuf, res,
     local_sem, halo_send, halo_recv, core_send, core_recv, y_send, y_recv, z_send, z_recv, x_send, x_recv,
 ):
@@ -86,6 +104,8 @@
         pltpu.make_async_copy(probe_in, probe, local_sem.at[1]),
         pltpu.make_async_copy(inten_in, inten, local_sem.at[2]),
         pltpu.make_async_copy(tab_in, tab, local_sem.at[3]),
+        pltpu.make_async_copy(row_turn_in, row_turn, local_sem.at[6]),
+        pltpu.make_async_copy(lane_turn_in, lane_turn, local_sem.at[7]),
     ]
     loads[1].start()
 
@@ -122,6 +142,8 @@
     loads[0].start()
     loads[2].start()
     loads[3].start()
+    loads[4].start()
+    loads[5].start()
     one = lambda flag: flag.astype(jnp.int32)
     pl.semaphore_wait(barrier, ny + nz + 1 + one(has_up) + one(has_down) + one(far_left) + one(far_right))
 
@@ -226,6 +248,23 @@
 
     lax.fori_loop(0, SLOTS, shift_probe, 0)
 
+    loads[2].wait()
+    line, lane = lax.broadcasted_iota(jnp.int32, (N, N), 0), lax.broadcasted_iota(jnp.int32, (N, N), 1)
+    sort_rows = one_hot(lane == jnp.where(line < M, 2 * line, 2 * line - (N - 1)))
+    sort_lanes = one_hot(line == jnp.where(lane < M, 2 * lane, 2 * lane - (N - 1)))
+
+    def sort_intensity(s, _):
+        high, low = split(inten[s])
+        Uc[:N, :] = dot(sort_rows, high).astype(bf16)
+        Uc[N:2 * N, :] = dot(sort_rows, low).astype(bf16)
+        a = dot(Uc[:2 * N, :], sort_lanes)
+        a = a[:N] + a[N:]
+        Ip[s, :, :N] = a[:M]
+        Ip[s, :, N:] = a[M:]
+        return 0
+
+    lax.fori_loop(0, SLOTS, sort_intensity, 0)
+
     @pl.when(has_right)
     def _():
         right_in[0].wait_recv()
@@ -235,7 +274,7 @@
         def _():
             corner_in.start()
 
-    for load in (loads[0], loads[2], loads[3]):
+    for load in (loads[0], loads[3], loads[4], loads[5]):
         load.wait()
 
     @pl.when(has_down)
@@ -263,50 +302,65 @@
             waves = (pr * parts[0] - pi * parts[1], pr * parts[1] + pi * parts[0])
             for q, wave in enumerate(waves):
                 ex[s, q, rows(i0, CH), :] = wave
-                high, low = split(wave)
-                X[s, rows(i0, CH), q * N:(q + 1) * N] = high
-                X[s, rows(i0 + N, CH), q * N:(q + 1) * N] = low
+            turn = (lane_turn[0, rows(i0, CH), :], lane_turn[1, rows(i0, CH), :])
+            pair = forward_half([w[:, :M] for w in waves], [w[:, M:] for w in waves], *turn)
+            for b in range(2):
+                for q in range(2):
+                    high, low = split(pair[b][q])
+                    X[s, rows(i0 + b * N, CH), q * M:(q + 1) * M] = high
+                    X[s, rows(i0 + (b + 2) * N, CH), q * M:(q + 1) * M] = low
             return 0
 
         lax.fori_loop(0, N // CH, gather, 0, unroll=8)
         a = dot(X[s], tab[0, 0])
-        a = a[:N] + a[N:] + dot(X[s, :N], tab[0, 1])
-        for q in range(2):
-            high, low = split(a[:, q * N:(q + 1) * N])
-            Y[s, q * N:(q + 1) * N, :N] = high
-            Y[s, q * N:(q + 1) * N, N:] = low
+        a = a[:2 * N] + a[2 * N:] + dot(X[s, :2 * N], tab[0, 1])
+        a = [jnp.concatenate([a[:N, q * M:(q + 1) * M], a[N:, q * M:(q + 1) * M]], axis=1) for q in range(2)]
+        pair = forward_half([w[:M] for w in a], [w[M:] for w in a], row_turn[0], row_turn[1])
+        for b in range(2):
+            for q in range(2):
+                high, low = split(pair[b][q])
+                Y[s, q * M:(q + 1) * M, b * N:(b + 1) * N] = high
+                Y[s, q * M:(q + 1) * M, (b + 2) * N:(b + 3) * N] = low
         a = dot(tab[1, 0], Y[s])
-        D[s] = a[:, :N] + a[:, N:] + dot(tab[1, 1], Y[s, :, :N])
+        D[s] = a[:, :2 * N] + a[:, 2 * N:] + dot(tab[1, 1], Y[s, :, :2 * N])
 
         def project(i, _):
-            i0 = i * CH
-            zr, zi = D[s, rows(i0, CH), :], D[s, rows(i0 + N, CH), :]
-            measured = inten[s, rows(i0, CH), :]
+            i0 = i * 16
+            zr, zi = D[s, rows(i0, 16), :], D[s, rows(i0 + M, 16), :]
+            measured = Ip[s, rows(i0, 16), :]
             factor = measured * lax.rsqrt(measured * (zr * zr + zi * zi + stabilizer))
             for q, wave in enumerate((zr * factor, zi * factor)):
                 high, low = split(wave)
-                Pj[s, rows(i0 + q * N, CH), :N] = high
-                Pj[s, rows(i0 + q * N, CH), N:] = low
+                there = pl.ds(pl.multiple_of(i0 + q * M, 16), 16)
+                Pj[s, there, :2 * N] = high
+                Pj[s, there, 2 * N:] = low
             return 0
 
-        lax.fori_loop(0, N // CH, project, 0, unroll=8)
+        lax.fori_loop(0, M // 16, project, 0, unroll=8)
         a = dot(tab[0, 0], Pj[s])
-        a = a[:, :N] + a[:, N:] + dot(tab[0, 1], Pj[s, :, :N])
-        for q in range(2):
-            high, low = split(a[q * N:(q + 1) * N])
-            X[s, :N, q * N:(q + 1) * N] = high
-            X[s, N:, q * N:(q + 1) * N] = low
+        a = a[:, :2 * N] + a[:, 2 * N:] + dot(tab[0, 1], Pj[s, :, :2 * N])
+        pair = backward_half((a[:M, :N], a[M:, :N]), (a[:M, N:], a[M:, N:]), row_turn[0], row_turn[1])
+        for b in range(2):
+            for q in range(2):
+                high, low = split(pair[b][q])
+                for part in range(2):
+                    there = slice(part * N + b * M, part * N + (b + 1) * M)
+                    below = slice((part + 2) * N + b * M, (part + 2) * N + (b + 1) * M)
+                    X[s, there, q * M:(q + 1) * M] = high[:, part * M:(part + 1) * M]
+                    X[s, below, q * M:(q + 1) * M] = low[:, part * M:(part + 1) * M]
         a = dot(X[s], tab[1, 0])
-        a = a[:N] + a[N:] + dot(X[s, :N], tab[1, 1])
-        D[s, :N] = a[:, :N]
-        D[s, N:] = a[:, N:]
+        a = a[:2 * N] + a[2 * N:] + dot(X[s, :2 * N], tab[1, 1])
+        pair = backward_half((a[:N, :M], a[:N, M:]), (a[N:, :M], a[N:, M:]), lane_turn[0], lane_turn[1])
+        for b in range(2):
+            for q in range(2):
+                B[q * N:(q + 1) * N, b * M:(b + 1) * M] = pair[b][q]
 
         def finish(i, _):
             i0 = i * CH
             here, below = rows(i0, CH), rows(i0 + N, CH)
             live = lvec[s]
-            dr = (ex[s, 0, here, :] - D[s, here, :]) * live
-            di = (ex[s, 1, here, :] - D[s, below, :]) * live
+            dr = (ex[s, 0, here, :] - B[here, :]) * live
+            di = (ex[s, 1, here, :] - B[below, :]) * live
             wr, wi = patch[s, 0, here, :], patch[s, 1, here, :]
             for q, term in enumerate((wr * dr + wi * di, wr * di - wi * dr)):
                 high, low = split(term)
@@ -500,13 +554,16 @@
     grad, probe_grad = pl.pallas_call(
         functools.partial(kernel, nrow, ncol),
         out_shape=[jax.ShapeDtypeStruct((2, TR, TC), f32), jax.ShapeDtypeStruct((2, N, N), f32)],
-        in_specs=[scalars, scalars] + [anywhere] * 4,
+        in_specs=[scalars, scalars] + [anywhere] * 6,
         out_specs=[anywhere, anywhere],
         scratch_shapes=[
             vmem((2, 2 * TR, TC + N), f32),
             vmem((2, N, N), f32),
             vmem((SLOTS, N, N), f32),
-            vmem((2, 2, 2 * N, 2 * N), bf16),
+            vmem((2, 2, N, N), bf16),
+            vmem((2, M, N), f32),
+            vmem((2, N, M), f32),
+            vmem((SLOTS, M, 2 * N), f32),
             vmem((SLOTS, N, N), bf16),
             vmem((SLOTS, N, N), bf16),
             vmem((SLOTS, N, N), bf16),
@@ -517,10 +574,11 @@
             vmem((SLOTS, 3, 8, N), f32),
             vmem((N, 4 * N), bf16),
             vmem((SLOTS, 2, N, N), f32),
-            vmem((SLOTS, 2 * N, 2 * N), bf16),
-            vmem((SLOTS, 2 * N, 2 * N), bf16),
-            vmem((SLOTS, 2 * N, 2 * N), bf16),
-            vmem((SLOTS, 2 * N, N), f32),
+            vmem((SLOTS, 4 * N, N), bf16),
+            vmem((SLOTS, N, 4 * N), bf16),
+            vmem((SLOTS, N, 4 * N), bf16),
+            vmem((SLOTS, N, 2 * N), f32),
+            vmem((2 * N, N), f32),
             vmem((SLOTS, 2, N, N), f32),
             vmem((SLOTS, 2, N, N), f32),
             vmem((N, 4 * N), bf16),
@@ -537,11 +595,11 @@
             vmem((ny, 8, 128), f32),
             vmem((4, 8, 128), f32),
             vmem((2, N, N), f32),
-            dma((6,)), dma((9,)), dma((9,)), dma((2,)), dma((2,)),
+            dma((8,)), dma((9,)), dma((9,)), dma((2,)), dma((2,)),
             dma((2 * ny,)), dma((2 * ny,)), dma((2 * nz,)), dma((2 * nz,)), dma((4,)), dma((4,)),
         ],
         compiler_params=pltpu.CompilerParams(collective_id=0, has_side_effects=True, vmem_limit_bytes=56 * 2**20),
-    )(offsets.T, counts, object_field, probe_field, intensity, jnp.asarray(dft_tables()))
+    )(offsets.T, counts, object_field, probe_field, intensity, jnp.asarray(dft_tables()), *(jnp.asarray(t) for t in twiddles()))
     return grad, probe_grad
 
 

time: 102 us -> 99.1 us (0.972)
  Pallas kernels: 97.2 us -> 94.5 us
    pallas_call x1, Pallas kernels: 97.2 us -> 94.5 us  [local(): pl.pallas_call(functools.partial(kernel, nrow, ncol), out_shape=[jax.Shap...]
where the time goes in v2:
time: 99.1 us; the launch traced here: 98.9 us
  Pallas kernels  94.5 us (95%)
  local copies, waits for them, and re-layouts  3.12 us (3%)
  between operations  1.29 us (1%)
    pallas_call x1, Pallas kernels, local(): pl.pallas_call(functools.partial(kernel, nrow, ncol), out_shape=[jax.Shap...  94.5 us
    unnamed x4, local copies, waits for them, and re-layouts  3.12 us

profile of v2, /device:TPU:1, one launch (start us, length us, event | category | flops | bytes accessed | tf_op | source)
XLA Modules:
  0.0 98.9 jit_solution(5101579435021704466)
XLA Ops:
  1.3 94.5 %shard_map.95 = (f32[2,256,512]{2,1,0:T(8,128)}, f32[2,256,256]{2,1,0:T(8,128)}) custom-call(s32[2,4]{1,0:T(2,128)} %bitcast.1, s32[1]{0:T(128)S(6)} %copy.12.cnt, f32[2,256,512]{2,1,0:T(8,128)} %obj.1, f32[2,256,256]{2,1,0:T(8,128)} %probe_in.1, f32[4,256,256]{2,1,0:T(8,128)} %inten_in.1, bf16[2,2,256,256]{3,2,1,0:T(8,128)(2,1)} %constant.6.clone.tab_in, ...), custom_call_target="tpu_custom_call" | custom-call | tf_op jit(solution)/shard_map/pallas_call | solution.py:554
  95.8 0.0 copy-start
  95.8 2.3 %copy.13 = f32[2,256,512]{2,1,0:T(8,128)} copy(f32[2,256,512]{2,1,0:T(8,128)} %get-tuple-element.4) | data formatting | bytes 2097152
  98.1 0.0 copy-done
  98.1 0.8 copy.14
Async XLA Ops:
  95.8 2.3 %copy-start = (f32[2,256,256]{2,1,0:T(8,128)S(1)}, f32[2,256,256]{2,1,0:T(8,128)}, u32[]{:S(2)}) copy-start(f32[2,256,256]{2,1,0:T(8,128)} %get-tuple-element.5) | copy-start | bytes 1572868

commit v3 on v2

--- a/solution.py
+++ b/solution.py
@@ -20,6 +20,7 @@
 SLOTS = 4
 CH = 32
 M = N // 2
+PARTS = 4
 
 
 def dft_tables():
@@ -159,19 +160,21 @@
     right_id = (row, lax.min(col + 1, ncol - 1))
     top, bottom = pl.ds(0, TR), pl.ds(TR, TR)
     main, side = pl.ds(0, TC), pl.ds(TC, N)
-    half = TR // 2
-    halves = (pl.ds(0, half), pl.ds(half, half))
+    step = TR // PARTS
+    strips = [pl.ds(b * step, step) for b in range(PARTS)]
+    lower_strips = [pl.ds(TR + b * step, step) for b in range(PARTS)]
     right_in = [
-        halo(0, obj.at[:, halves[0], pl.ds(0, N)], ext.at[:, halves[0], side], left_id),
-        halo(6, obj.at[:, halves[1], pl.ds(0, N)], ext.at[:, halves[1], side], left_id),
+        halo(2 + b, obj.at[:, strips[b], pl.ds(0, N)], ext.at[:, strips[b], side], left_id) for b in range(PARTS)
     ]
-    lower_in = halo(1, obj, ext.at[:, bottom, main], up_id)
-    corner_in = halo(2, ext.at[:, top, side], ext.at[:, bottom, side], up_id)
+    corner_in = [
+        halo(2 + PARTS + b, ext.at[:, strips[b], side], ext.at[:, lower_strips[b], side], up_id) for b in range(PARTS)
+    ]
+    lower_in = halo(0, obj, ext.at[:, bottom, main], up_id)
 
     @pl.when(has_left)
     def _():
-        right_in[0].start()
-        right_in[1].start()
+        for copy in right_in:
+            copy.start()
 
     @pl.when(has_up)
     def _():
@@ -267,12 +270,12 @@
 
     @pl.when(has_right)
     def _():
-        right_in[0].wait_recv()
-        right_in[1].wait_recv()
-
-        @pl.when(has_up)
-        def _():
-            corner_in.start()
+        for b in range(PARTS):
+            right_in[b].wait_recv()
+
+            @pl.when(has_up)
+            def _():
+                corner_in[b].start()
 
     for load in (loads[0], loads[3], loads[4], loads[5]):
         load.wait()
@@ -283,7 +286,8 @@
 
         @pl.when(has_right)
         def _():
-            corner_in.wait_recv()
+            for copy in corner_in:
+                copy.wait_recv()
 
     def slot(s, _):
         def gather(i, _):
@@ -384,7 +388,7 @@
         return 0
 
     pgl[...] = jnp.zeros_like(pgl)
-    lax.fori_loop(0, SLOTS, slot, 0)
+    lax.fori_loop(0, SLOTS, slot, 0, unroll=2)
 
     def remote(source, target, send, recv, device):
         return pltpu.make_async_remote_copy(
@@ -409,16 +413,18 @@
 
     lax.fori_loop(0, N // 8, deposit, 0, unroll=4)
 
-    corner_out = halo(3, G.at[:, bottom, side], kbuf, down_id)
-    lower_out = halo(4, G.at[:, bottom, main], lbuf, down_id)
+    corner_out = [
+        halo(2 + 2 * PARTS + b, G.at[:, lower_strips[b], side], kbuf.at[:, strips[b], :], down_id) for b in range(PARTS)
+    ]
     right_out = [
-        halo(5, G.at[:, halves[0], side], rbuf.at[:, halves[0], :], right_id),
-        halo(8, G.at[:, halves[1], side], rbuf.at[:, halves[1], :], right_id),
+        halo(2 + 3 * PARTS + b, G.at[:, strips[b], side], rbuf.at[:, strips[b], :], right_id) for b in range(PARTS)
     ]
+    lower_out = halo(1, G.at[:, bottom, main], lbuf, down_id)
 
     @pl.when(has_down)
     def _():
-        corner_out.start()
+        for copy in corner_out:
+            copy.start()
         lower_out.start()
 
     to_partner.wait_recv()
@@ -445,21 +451,24 @@
     y_out = [remote(ysrc.at[y_peer(k)], yrecv.at[k], y_send.at[k], y_recv.at[k], y_id(k)) for k in range(1, ny)]
     for copy in y_out:
         copy.start()
-    @pl.when(has_up)
-    def _():
-        corner_out.wait_recv()
-
     def add_corner(i, _):
         for q in range(2):
             G[q, rows(i * CH, CH), TC:] += kbuf[q, rows(i * CH, CH), :]
         return 0
 
-    lax.fori_loop(0, TR // CH, add_corner, 0, unroll=8)
-
-    @pl.when(has_right)
-    def _():
-        right_out[0].start()
-        right_out[1].start()
+    def pass_corner(b):
+        @pl.when(has_up)
+        def _():
+            corner_out[b].wait_recv()
+
+        lax.fori_loop(b * step // CH, (b + 1) * step // CH, add_corner, 0, unroll=True)
+
+        @pl.when(has_right)
+        def _():
+            right_out[b].start()
+
+    for b in range(PARTS):
+        pass_corner(b)
 
     for copy in y_out:
         copy.wait_recv()
@@ -497,8 +506,8 @@
 
     @pl.when(has_left)
     def _():
-        right_out[0].wait_recv()
-        right_out[1].wait_recv()
+        for copy in right_out:
+            copy.wait_recv()
 
     def add_halos(i, _):
         here = rows(i * CH, CH)
@@ -516,8 +525,8 @@
 
     @pl.when(has_left)
     def _():
-        right_in[0].wait_send()
-        right_in[1].wait_send()
+        for copy in right_in:
+            copy.wait_send()
 
     @pl.when(has_up)
     def _():
@@ -525,17 +534,19 @@
 
         @pl.when(has_right)
         def _():
-            corner_in.wait_send()
+            for copy in corner_in:
+                copy.wait_send()
 
     @pl.when(has_down)
     def _():
-        corner_out.wait_send()
+        for copy in corner_out:
+            copy.wait_send()
         lower_out.wait_send()
 
     @pl.when(has_right)
     def _():
-        right_out[0].wait_send()
-        right_out[1].wait_send()
+        for copy in right_out:
+            copy.wait_send()
 
     to_partner.wait_send()
     share.wait_send()
@@ -595,7 +606,7 @@
             vmem((ny, 8, 128), f32),
             vmem((4, 8, 128), f32),
             vmem((2, N, N), f32),
-            dma((8,)), dma((9,)), dma((9,)), dma((2,)), dma((2,)),
+            dma((8,)), dma((2 + 4 * PARTS,)), dma((2 + 4 * PARTS,)), dma((2,)), dma((2,)),
             dma((2 * ny,)), dma((2 * ny,)), dma((2 * nz,)), dma((2 * nz,)), dma((4,)), dma((4,)),
         ],
         compiler_params=pltpu.CompilerParams(collective_id=0, has_side_effects=True, vmem_limit_bytes=56 * 2**20),

time: 99.1 us -> 93.9 us (0.948)
  Pallas kernels: 94.5 us -> 88.3 us
    pallas_call x1, Pallas kernels: 94.5 us -> 88.3 us  [local(): pl.pallas_call(functools.partial(kernel, nrow, ncol), out_shape=[jax.Shap...]
where the time goes in v3:
time: 93.9 us; the launch traced here: 92.7 us
  Pallas kernels  88.3 us (94%)
  local copies, waits for them, and re-layouts  3.12 us (3%)
  between operations  1.29 us (1%)
    pallas_call x1, Pallas kernels, local(): pl.pallas_call(functools.partial(kernel, nrow, ncol), out_shape=[jax.Shap...  88.3 us
    unnamed x4, local copies, waits for them, and re-layouts  3.12 us

profile of v3, /device:TPU:1, one launch (start us, length us, event | category | flops | bytes accessed | tf_op | source)
XLA Modules:
  0.0 92.7 jit_solution(12737281446698139110)
XLA Ops:
  1.3 88.3 %shard_map.95 = (f32[2,256,512]{2,1,0:T(8,128)}, f32[2,256,256]{2,1,0:T(8,128)}) custom-call(s32[2,4]{1,0:T(2,128)} %bitcast.1, s32[1]{0:T(128)S(6)} %copy.12.cnt, f32[2,256,512]{2,1,0:T(8,128)} %obj.1, f32[2,256,256]{2,1,0:T(8,128)} %probe_in.1, f32[4,256,256]{2,1,0:T(8,128)} %inten_in.1, bf16[2,2,256,256]{3,2,1,0:T(8,128)(2,1)} %constant.6.clone.tab_in, ...), custom_call_target="tpu_custom_call" | custom-call | tf_op jit(solution)/shard_map/pallas_call | solution.py:565
  89.6 0.0 copy-start
  89.6 2.3 %copy.13 = f32[2,256,512]{2,1,0:T(8,128)} copy(f32[2,256,512]{2,1,0:T(8,128)} %get-tuple-element.4) | data formatting | bytes 2097152
  91.9 0.0 copy-done
  91.9 0.8 copy.14
Async XLA Ops:
  89.6 2.3 %copy-start = (f32[2,256,256]{2,1,0:T(8,128)S(1)}, f32[2,256,256]{2,1,0:T(8,128)}, u32[]{:S(2)}) copy-start(f32[2,256,256]{2,1,0:T(8,128)} %get-tuple-element.5) | copy-start | bytes 1572868

commit v4 on v3

--- a/solution.py
+++ b/solution.py
@@ -495,10 +495,14 @@
     y_back = [remote(res.at[my_rows], res.at[my_rows], y_send.at[ny + k], y_recv.at[ny + k], y_id(k)) for k in range(1, ny)]
     for copy in y_back:
         copy.start()
-    for copy in y_back:
-        copy.wait_recv()
-    share = remote(res.at[core], res.at[core], core_send.at[1], core_recv.at[1], (partner, col))
-    share.start()
+    shares = []
+    for k in range(ny):
+        if k > 0:
+            y_back[k - 1].wait_recv()
+        owner = lax.rem(y - k + ny, ny)
+        piece = res.at[core, rows(8 * nz * (owner // 2), 8 * nz), pl.ds(pl.multiple_of(128 * (owner % 2), 128), 128)]
+        shares.append(remote(piece, piece, core_send.at[1 + k], core_recv.at[1 + k], (partner, col)))
+        shares[k].start()
 
     @pl.when(has_up)
     def _():
@@ -519,7 +523,8 @@
     lax.fori_loop(0, TR // CH, add_halos, 0, unroll=8)
     store_grad = pltpu.make_async_copy(G.at[:, top, main], grad_out, local_sem.at[4])
     store_grad.start()
-    share.wait_recv()
+    for copy in shares:
+        copy.wait_recv()
     store_probe = pltpu.make_async_copy(res, pg_out, local_sem.at[5])
     store_probe.start()
 
@@ -549,7 +554,8 @@
             copy.wait_send()
 
     to_partner.wait_send()
-    share.wait_send()
+    for copy in shares:
+        copy.wait_send()
     for copy in y_out + z_out + x_out + z_back + y_back:
         copy.wait_send()
     store_grad.wait()
@@ -606,7 +612,7 @@
             vmem((ny, 8, 128), f32),
             vmem((4, 8, 128), f32),
             vmem((2, N, N), f32),
-            dma((8,)), dma((2 + 4 * PARTS,)), dma((2 + 4 * PARTS,)), dma((2,)), dma((2,)),
+            dma((8,)), dma((2 + 4 * PARTS,)), dma((2 + 4 * PARTS,)), dma((9,)), dma((9,)),
             dma((2 * ny,)), dma((2 * ny,)), dma((2 * nz,)), dma((2 * nz,)), dma((4,)), dma((4,)),
         ],
         compiler_params=pltpu.CompilerParams(collective_id=0, has_side_effects=True, vmem_limit_bytes=56 * 2**20),

time: 93.9 us -> 93.9 us (level)
  no operation moved by 1% of the time
where the time goes in v4:
time: 93.9 us; the launch traced here: 92.8 us
  Pallas kernels  88.4 us (94%)
  local copies, waits for them, and re-layouts  3.12 us (3%)
  between operations  1.29 us (1%)
    pallas_call x1, Pallas kernels, local(): pl.pallas_call(functools.partial(kernel, nrow, ncol), out_shape=[jax.Shap...  88.4 us
    unnamed x4, local copies, waits for them, and re-layouts  3.12 us

profile of v4, /device:TPU:1, one launch (start us, length us, event | category | flops | bytes accessed | tf_op | source)
XLA Modules:
  0.0 92.8 jit_solution(1260139144622425001)
XLA Ops:
  1.3 88.4 %shard_map.95 = (f32[2,256,512]{2,1,0:T(8,128)}, f32[2,256,256]{2,1,0:T(8,128)}) custom-call(s32[2,4]{1,0:T(2,128)} %bitcast.1, s32[1]{0:T(128)S(6)} %copy.12.cnt, f32[2,256,512]{2,1,0:T(8,128)} %obj.1, f32[2,256,256]{2,1,0:T(8,128)} %probe_in.1, f32[4,256,256]{2,1,0:T(8,128)} %inten_in.1, bf16[2,2,256,256]{3,2,1,0:T(8,128)(2,1)} %constant.6.clone.tab_in, ...), custom_call_target="tpu_custom_call" | custom-call | tf_op jit(solution)/shard_map/pallas_call | solution.py:571
  89.7 0.0 copy-start
  89.7 2.3 %copy.13 = f32[2,256,512]{2,1,0:T(8,128)} copy(f32[2,256,512]{2,1,0:T(8,128)} %get-tuple-element.4) | data formatting | bytes 2097152
  92.0 0.0 copy-done
  92.0 0.8 copy.14
Async XLA Ops:
  89.7 2.3 %copy-start = (f32[2,256,256]{2,1,0:T(8,128)S(1)}, f32[2,256,256]{2,1,0:T(8,128)}, u32[]{:S(2)}) copy-start(f32[2,256,256]{2,1,0:T(8,128)} %get-tuple-element.5) | copy-start | bytes 1572868
